TPU v7x, 128 devices: a whole 4x4x4 slice. The times are simulated.
128 devices in a mesh: tm: 4 (over y_hi, core), head: 32 (over x, y_lo, z).
Axes of the slice: x: 4, y: 4 (y_hi: 2, y_lo: 2; y = y_hi * 2 + y_lo), z: 4, core: 2. Of those that a mesh axis runs over, the one named last changes fastest.
Arguments:
- query: bfloat16 [8, 2048, 4096], P('tm', 'head'), may hold values from -5 to 5
- key_in: bfloat16 [8, 2048, 4096], P('tm', 'head'), may hold values from -5 to 5
- value: bfloat16 [8, 2048, 4096], P('tm', 'head'), may hold values from -6 to 6
- query_dot: bfloat16 [8, 2048, 4096], P('tm', 'head'), may hold values from -6 to 6
- key_dot: bfloat16 [8, 2048, 4096], P('tm', 'head'), may hold values from -6 to 6
- value_dot: bfloat16 [8, 2048, 4096], P('tm', 'head'), may hold values from -6 to 6
Outputs:
- attended: bfloat16 [8, 2048, 4096], P('tm', 'head')
- attended_dot: bfloat16 [8, 2048, 4096], P('tm', 'head')
All inputs are finite; a program needn't handle non-finite values.
Results may differ from a plain program's by a relative error of at most 0.0049.
Values may be sent and summed in bfloat16 or wider, within the bound.
A program may use at most 128 MiB of HBM per device.

v0:
```python
import math

import jax
import jax.numpy as jnp
from jax import lax
from jax.sharding import PartitionSpec as P

HD = 128


def from_behind(block, axis, distance):
    devices = range(lax.axis_size(axis))
    route = [(i - distance, i) for i in devices if i - distance in devices]
    return lax.ppermute(block, axis, route)


def contract(left, right):
    return lax.dot_general(
        left, right, (((1,), (1,)), ((), ())), preferred_element_type=jnp.float32
    )


def attend_block(query_b, query_dot_b, keys, values, keys_dot, values_dot, prior_ok):
    width = keys.shape[0] // 2
    factor = 1.0 / math.sqrt(query_b.shape[1])
    scores = contract(query_b, keys) * factor
    scores_dot = (contract(query_dot_b, keys) + contract(query_b, keys_dot)) * factor
    valid = (jnp.arange(2 * width) >= width) | prior_ok
    scores = jnp.where(valid[None, :], scores, -1e30)
    top = jnp.max(scores, axis=1, keepdims=True)
    weights = jnp.exp(scores - top)
    probs = weights / jnp.sum(weights, axis=1, keepdims=True)
    mean_dot = jnp.sum(probs * scores_dot, axis=1, keepdims=True)
    probs_dot = probs * (scores_dot - mean_dot)
    probs_low = probs.astype(jnp.bfloat16)
    probs_dot_low = probs_dot.astype(jnp.bfloat16)
    output = jnp.dot(probs_low, values, preferred_element_type=jnp.float32)
    output_dot = jnp.dot(probs_dot_low, values, preferred_element_type=jnp.float32) + jnp.dot(
        probs_low, values_dot, preferred_element_type=jnp.float32
    )
    return (output.astype(jnp.bfloat16), output_dot.astype(jnp.bfloat16))


def attend_frame(query_f, query_dot_f, keys, values, keys_dot, values_dot, prior_ok):
    width, size = query_f.shape
    block = math.gcd(width, 512)
    count = width // block
    blocks = (query_f.reshape(count, block, size), query_dot_f.reshape(count, block, size))
    output, output_dot = lax.map(
        lambda part: attend_block(part[0], part[1], keys, values, keys_dot, values_dot, prior_ok),
        blocks,
    )
    return (output.reshape(width, size), output_dot.reshape(width, size))


def to_heads(query, query_dot, keys, values, keys_dot, values_dot):
    moved = (
        lax.all_to_all(query, "head", split_axis=2, concat_axis=1, tiled=True),
        lax.all_to_all(query_dot, "head", split_axis=2, concat_axis=1, tiled=True),
        lax.all_to_all(keys, "head", split_axis=2, concat_axis=1, tiled=True),
        lax.all_to_all(values, "head", split_axis=2, concat_axis=1, tiled=True),
        lax.all_to_all(keys_dot, "head", split_axis=2, concat_axis=1, tiled=True),
        lax.all_to_all(values_dot, "head", split_axis=2, concat_axis=1, tiled=True),
    )
    return moved


def per_device(query, key_in, value, query_dot, key_dot, value_dot):
    frames = query.shape[0]
    prior = from_behind((key_in[-1:], value[-1:], key_dot[-1:], value_dot[-1:]), "tm", 1)
    joined = [
        jnp.concatenate([first, rest], axis=0)
        for first, rest in zip(prior, (key_in, value, key_dot, value_dot))
    ]
    q_heads, qd_heads, k_heads, v_heads, kd_heads, vd_heads = to_heads(
        query, query_dot, joined[0], joined[1], joined[2], joined[3]
    )
    width = q_heads.shape[1]
    local = q_heads.shape[2] // HD

    def split(array):
        return array.reshape(array.shape[0], width, local, HD).transpose(0, 2, 1, 3)

    q_split, qd_split = (split(q_heads), split(qd_heads))
    k_split, v_split = (split(k_heads), split(v_heads))
    kd_split, vd_split = (split(kd_heads), split(vd_heads))
    later_device = lax.axis_index("tm") > 0

    def one_frame(index):
        prior_ok = (index > 0) | later_device

        def joined_keys(array):
            return jnp.concatenate([array[index], array[index + 1]], axis=1)

        items = (
            q_split[index],
            qd_split[index],
            joined_keys(k_split),
            joined_keys(v_split),
            joined_keys(kd_split),
            joined_keys(vd_split),
        )
        return lax.map(lambda part: attend_frame(*part, prior_ok), items)

    output, output_dot = lax.map(one_frame, jnp.arange(frames))

    def merge(array):
        return array.transpose(0, 2, 1, 3).reshape(frames, width, local * HD)

    result = (
        lax.all_to_all(merge(output), "head", split_axis=1, concat_axis=2, tiled=True),
        lax.all_to_all(merge(output_dot), "head", split_axis=1, concat_axis=2, tiled=True),
    )
    return (result[0], result[1])


def solution(mesh):
    in_specs = (
        P("tm", "head", None),
        P("tm", "head", None),
        P("tm", "head", None),
        P("tm", "head", None),
        P("tm", "head", None),
        P("tm", "head", None),
    )
    out_specs = (P("tm", "head", None), P("tm", "head", None))
    return jax.shard_map(
        per_device, mesh=mesh, in_specs=in_specs, out_specs=out_specs, check_vma=False
    )
```

profile of v0, /device:TPU:16, one launch (start us, length us, event | category | flops | bytes accessed | tf_op | source)
XLA Modules:
  0.0 547.9 jit_solution(7247275522706363583)
XLA Ops:
  7.9 8.9 %all-to-all-start = ((bf16[32,2,8192]{2,1,0:T(2,128)(2,1)}), bf16[32,2,8192]{2,1,0:T(2,128)(2,1)S(1)}, u32[]{:S(2)}, u32[]{:S(2)}) async-start(bf16[32,2,8192]{2,1,0:T(2,128)(2,1)} %reshape.44), calls=%async_computation | async-start | bytes 2097152 | tf_op jit(solution)/shard_map/all_to_all | solution.py:58
  24.1 9.2 %all-to-all-done = bf16[32,2,8192]{2,1,0:T(2,128)(2,1)S(1)} async-done(((bf16[32,2,8192]{2,1,0:T(2,128)(2,1)}), bf16[32,2,8192]{2,1,0:T(2,128)(2,1)S(1)}, u32[]{:S(2)}, u32[]{:S(2)}) %all-to-all-start) | async-done | bytes 1048608 | tf_op jit(solution)/shard_map/all_to_all | solution.py:58
  41.1 14.9 %collective-permute-done = bf16[1,64,4096]{2,1,0:T(8,128)(2,1)S(1)} collective-permute-done((bf16[1,64,4096]{2,1,0:T(8,128)(2,1)S(1)}, bf16[1,64,4096]{2,1,0:T(8,128)(2,1)S(1)}, u32[]{:S(2)}, u32[]{:S(2)}) %collective-permute-start) | collective-permute-done | bytes 524320 | tf_op jit(solution)/shard_map/ppermute | solution.py:14
  62.1 7.4 %reshape.48 = bf16[32,2,12288]{2,1,0:T(2,128)(2,1)} reshape(bf16[4096,3,64]{2,1,0:T(4,128)(2,1)} %bitcast.153) | data formatting | bytes 3145728
  69.5 8.0 %all-to-all-start.2 = ((bf16[32,2,12288]{2,1,0:T(2,128)(2,1)}), bf16[32,2,12288]{2,1,0:T(2,128)(2,1)S(1)}, u32[]{:S(2)}, u32[]{:S(2)}) async-start(bf16[32,2,12288]{2,1,0:T(2,128)(2,1)} %reshape.48), calls=%async_computation.2 | async-start | bytes 3145728 | tf_op jit(solution)/shard_map/all_to_all | solution.py:60
  79.5 12.9 %collective-permute-done.1 = bf16[1,64,4096]{2,1,0:T(8,128)(2,1)S(1)} collective-permute-done((bf16[1,64,4096]{2,1,0:T(8,128)(2,1)S(1)}, bf16[1,64,4096]{2,1,0:T(8,128)(2,1)S(1)}, u32[]{:S(2)}, u32[]{:S(2)}) %collective-permute-start.1) | collective-permute-done | bytes 524320 | tf_op jit(solution)/shard_map/ppermute | solution.py:14
  98.6 7.2 %reshape.50 = bf16[32,2,12288]{2,1,0:T(2,128)(2,1)} reshape(bf16[4096,3,64]{2,1,0:T(4,128)(2,1)} %bitcast.154) | data formatting | bytes 3145728
  105.8 7.8 %all-to-all-start.3 = ((bf16[32,2,12288]{2,1,0:T(2,128)(2,1)}), bf16[32,2,12288]{2,1,0:T(2,128)(2,1)S(1)}, u32[]{:S(2)}, u32[]{:S(2)}) async-start(bf16[32,2,12288]{2,1,0:T(2,128)(2,1)} %reshape.50), calls=%async_computation.3 | async-start | bytes 3145728 | tf_op jit(solution)/shard_map/all_to_all | solution.py:62
  116.6 11.9 %collective-permute-done.2 = bf16[1,64,4096]{2,1,0:T(8,128)(2,1)S(1)} collective-permute-done((bf16[1,64,4096]{2,1,0:T(8,128)(2,1)S(1)}, bf16[1,64,4096]{2,1,0:T(8,128)(2,1)S(1)}, u32[]{:S(2)}, u32[]{:S(2)}) %collective-permute-start.2) | collective-permute-done | bytes 524320 | tf_op jit(solution)/shard_map/ppermute | solution.py:14
  137.5 7.2 %reshape.52 = bf16[32,2,12288]{2,1,0:T(2,128)(2,1)} reshape(bf16[4096,3,64]{2,1,0:T(4,128)(2,1)} %bitcast.155) | data formatting | bytes 3145728
  144.7 7.8 %all-to-all-start.4 = ((bf16[32,2,12288]{2,1,0:T(2,128)(2,1)}), bf16[32,2,12288]{2,1,0:T(2,128)(2,1)S(1)}, u32[]{:S(2)}, u32[]{:S(2)}) async-start(bf16[32,2,12288]{2,1,0:T(2,128)(2,1)} %reshape.52), calls=%async_computation.4 | async-start | bytes 3145728 | tf_op jit(solution)/shard_map/all_to_all | solution.py:61
  155.6 11.9 %collective-permute-done.3 = bf16[1,64,4096]{2,1,0:T(8,128)(2,1)S(1)} collective-permute-done((bf16[1,64,4096]{2,1,0:T(8,128)(2,1)S(1)}, bf16[1,64,4096]{2,1,0:T(8,128)(2,1)S(1)}, u32[]{:S(2)}, u32[]{:S(2)}) %collective-permute-start.3) | collective-permute-done | bytes 524320 | tf_op jit(solution)/shard_map/ppermute | solution.py:14
  176.4 7.3 %reshape.54 = bf16[32,2,12288]{2,1,0:T(2,128)(2,1)} reshape(bf16[4096,3,64]{2,1,0:T(4,128)(2,1)} %bitcast.156) | data formatting | bytes 3145728
  183.7 8.0 %all-to-all-start.5 = ((bf16[32,2,12288]{2,1,0:T(2,128)(2,1)}), bf16[32,2,12288]{2,1,0:T(2,128)(2,1)}, u32[]{:S(2)}, u32[]{:S(2)}) async-start(bf16[32,2,12288]{2,1,0:T(2,128)(2,1)} %reshape.54), calls=%async_computation.5 | async-start | bytes 3145728 | tf_op jit(solution)/shard_map/all_to_all | solution.py:63
  205.8 7.1 %reshape.49 = bf16[4096,3,64]{2,1,0:T(4,128)(2,1)} reshape(bf16[32,2,12288]{2,1,0:T(2,128)(2,1)} %copy-done.1) | data formatting | bytes 3145728
  212.9 6.4 %copy.41 = bf16[3,32,64,128]{3,2,1,0:T(8,128)(2,1)} copy(bf16[3,32,64,128]{2,0,3,1:T(4,128)(2,1)} %bitcast.157) | data formatting | bytes 3145728 | tf_op jit(solution)/shard_map/all_to_all | solution.py:60
  224.1 6.4 %copy.43 = bf16[3,32,64,128]{3,2,1,0:T(8,128)(2,1)} copy(bf16[3,32,64,128]{2,0,3,1:T(4,128)(2,1)} %bitcast.158) | data formatting | bytes 3145728 | tf_op jit(solution)/shard_map/all_to_all | solution.py:62
  241.6 7.1 %reshape.55 = bf16[4096,3,64]{2,1,0:T(4,128)(2,1)} reshape(bf16[32,2,12288]{2,1,0:T(2,128)(2,1)} %all-to-all-done.5) | data formatting | bytes 3145728
  255.5 248.3 %while.48 = (s32[]{:T(128)}, bf16[2,1,2048,128]{3,2,1,0:T(8,128)(2,1)}, bf16[2,1,2048,128]{3,2,1,0:T(8,128)(2,1)}, s32[2]{0:T(128)}, bf16[2,1,2048,128]{3,2,1,0:...) while((s32[]{:T(128)}, ...), condition=%wide.region_6.7_spmd, body=%wide.region_0.6_spmd.sunk | while | flops 3271760384 | bytes 124945944 | solution.py:105
  269.5 106.4 %while.49 = (s32[]{:T(128)}, bf16[4,512,128]{2,1,0:T(8,128)(2,1)}, bf16[4,512,128]{2,1,0:T(8,128)(2,1)}, pred[]{:T(512)}, bf16[4,512,128]{2,1,0:T(8,128)(2,1)}, ...) while((s32[]{:T(128)}, bf16[4,512,128]{2,1,0:T(8,128)(2,1)}, ...), condition=%wide.region_5.5_spmd, body=%wide.region_1.4_spmd.sunk | while | flops 3263371776 | bytes 103973000 | solution.py:49
  278.6 8.7 %multiply_reduce_fusion.2 = (f32[512]{0:T(512)S(1)}, f32[512,4096]{1,0:T(8,128)S(1)}, f32[512,4096]{1,0:T(8,128)}) fusion(f32[512]{0:T(512)S(1)} %fusion.76, f32[512]{0:T(512)S(1)} %get-tuple-element.465, f32[512,4096]{1,0:T(8,128)S(1)} %get-tuple-element.464, pred[4096]{0:T(1024)(128)(4,1)S(1)} %fusion.74, f32[512,4096]{1,0:T(8,128)} %fusion.77, ...), kind=kOutput, calls=%fused_computation.1.clone.1 | convolution fusion | flops 553647616 | bytes 34744832 | tf_op jit(solution)/shard_map/while/body/eval_jaxpr/while/body/eval_jaxpr/while/body/eval_jaxpr/dot_general | solution.py:18
  305.2 8.7 %multiply_reduce_fusion.2 = (f32[512]{0:T(512)S(1)}, f32[512,4096]{1,0:T(8,128)S(1)}, f32[512,4096]{1,0:T(8,128)}) fusion(f32[512]{0:T(512)S(1)} %fusion.76, f32[512]{0:T(512)S(1)} %get-tuple-element.465, f32[512,4096]{1,0:T(8,128)S(1)} %get-tuple-element.464, pred[4096]{0:T(1024)(128)(4,1)S(1)} %fusion.74, f32[512,4096]{1,0:T(8,128)} %fusion.77, ...), kind=kOutput, calls=%fused_computation.1.clone.1 | convolution fusion | flops 553647616 | bytes 34744832 | tf_op jit(solution)/shard_map/while/body/eval_jaxpr/while/body/eval_jaxpr/while/body/eval_jaxpr/dot_general | solution.py:18
  331.8 8.7 %multiply_reduce_fusion.2 = (f32[512]{0:T(512)S(1)}, f32[512,4096]{1,0:T(8,128)S(1)}, f32[512,4096]{1,0:T(8,128)}) fusion(f32[512]{0:T(512)S(1)} %fusion.76, f32[512]{0:T(512)S(1)} %get-tuple-element.465, f32[512,4096]{1,0:T(8,128)S(1)} %get-tuple-element.464, pred[4096]{0:T(1024)(128)(4,1)S(1)} %fusion.74, f32[512,4096]{1,0:T(8,128)} %fusion.77, ...), kind=kOutput, calls=%fused_computation.1.clone.1 | convolution fusion | flops 553647616 | bytes 34744832 | tf_op jit(solution)/shard_map/while/body/eval_jaxpr/while/body/eval_jaxpr/while/body/eval_jaxpr/dot_general | solution.py:18
  358.4 8.7 %multiply_reduce_fusion.2 = (f32[512]{0:T(512)S(1)}, f32[512,4096]{1,0:T(8,128)S(1)}, f32[512,4096]{1,0:T(8,128)}) fusion(f32[512]{0:T(512)S(1)} %fusion.76, f32[512]{0:T(512)S(1)} %get-tuple-element.465, f32[512,4096]{1,0:T(8,128)S(1)} %get-tuple-element.464, pred[4096]{0:T(1024)(128)(4,1)S(1)} %fusion.74, f32[512,4096]{1,0:T(8,128)} %fusion.77, ...), kind=kOutput, calls=%fused_computation.1.clone.1 | convolution fusion | flops 553647616 | bytes 34744832 | tf_op jit(solution)/shard_map/while/body/eval_jaxpr/while/body/eval_jaxpr/while/body/eval_jaxpr/dot_general | solution.py:18
  393.7 106.4 %while.49 = (s32[]{:T(128)}, bf16[4,512,128]{2,1,0:T(8,128)(2,1)}, bf16[4,512,128]{2,1,0:T(8,128)(2,1)}, pred[]{:T(512)}, bf16[4,512,128]{2,1,0:T(8,128)(2,1)}, ...) while((s32[]{:T(128)}, bf16[4,512,128]{2,1,0:T(8,128)(2,1)}, ...), condition=%wide.region_5.5_spmd, body=%wide.region_1.4_spmd.sunk | while | flops 3263371776 | bytes 103973000 | solution.py:49
  402.8 8.7 %multiply_reduce_fusion.2 = (f32[512]{0:T(512)S(1)}, f32[512,4096]{1,0:T(8,128)S(1)}, f32[512,4096]{1,0:T(8,128)}) fusion(f32[512]{0:T(512)S(1)} %fusion.76, f32[512]{0:T(512)S(1)} %get-tuple-element.465, f32[512,4096]{1,0:T(8,128)S(1)} %get-tuple-element.464, pred[4096]{0:T(1024)(128)(4,1)S(1)} %fusion.74, f32[512,4096]{1,0:T(8,128)} %fusion.77, ...), kind=kOutput, calls=%fused_computation.1.clone.1 | convolution fusion | flops 553647616 | bytes 34744832 | tf_op jit(solution)/shard_map/while/body/eval_jaxpr/while/body/eval_jaxpr/while/body/eval_jaxpr/dot_general | solution.py:18
  429.4 8.7 %multiply_reduce_fusion.2 = (f32[512]{0:T(512)S(1)}, f32[512,4096]{1,0:T(8,128)S(1)}, f32[512,4096]{1,0:T(8,128)}) fusion(f32[512]{0:T(512)S(1)} %fusion.76, f32[512]{0:T(512)S(1)} %get-tuple-element.465, f32[512,4096]{1,0:T(8,128)S(1)} %get-tuple-element.464, pred[4096]{0:T(1024)(128)(4,1)S(1)} %fusion.74, f32[512,4096]{1,0:T(8,128)} %fusion.77, ...), kind=kOutput, calls=%fused_computation.1.clone.1 | convolution fusion | flops 553647616 | bytes 34744832 | tf_op jit(solution)/shard_map/while/body/eval_jaxpr/while/body/eval_jaxpr/while/body/eval_jaxpr/dot_general | solution.py:18
  456.0 8.7 %multiply_reduce_fusion.2 = (f32[512]{0:T(512)S(1)}, f32[512,4096]{1,0:T(8,128)S(1)}, f32[512,4096]{1,0:T(8,128)}) fusion(f32[512]{0:T(512)S(1)} %fusion.76, f32[512]{0:T(512)S(1)} %get-tuple-element.465, f32[512,4096]{1,0:T(8,128)S(1)} %get-tuple-element.464, pred[4096]{0:T(1024)(128)(4,1)S(1)} %fusion.74, f32[512,4096]{1,0:T(8,128)} %fusion.77, ...), kind=kOutput, calls=%fused_computation.1.clone.1 | convolution fusion | flops 553647616 | bytes 34744832 | tf_op jit(solution)/shard_map/while/body/eval_jaxpr/while/body/eval_jaxpr/while/body/eval_jaxpr/dot_general | solution.py:18
  482.6 8.7 %multiply_reduce_fusion.2 = (f32[512]{0:T(512)S(1)}, f32[512,4096]{1,0:T(8,128)S(1)}, f32[512,4096]{1,0:T(8,128)}) fusion(f32[512]{0:T(512)S(1)} %fusion.76, f32[512]{0:T(512)S(1)} %get-tuple-element.465, f32[512,4096]{1,0:T(8,128)S(1)} %get-tuple-element.464, pred[4096]{0:T(1024)(128)(4,1)S(1)} %fusion.74, f32[512,4096]{1,0:T(8,128)} %fusion.77, ...), kind=kOutput, calls=%fused_computation.1.clone.1 | convolution fusion | flops 553647616 | bytes 34744832 | tf_op jit(solution)/shard_map/while/body/eval_jaxpr/while/body/eval_jaxpr/while/body/eval_jaxpr/dot_general | solution.py:18
  507.6 8.3 %all-to-all-start.6 = ((bf16[2,2048,128]{2,0,1:T(2,128)(2,1)}), bf16[2,2048,128]{2,0,1:T(2,128)(2,1)S(1)}, u32[]{:S(2)}, u32[]{:S(2)}) async-start(bf16[2,2048,128]{2,0,1:T(2,128)(2,1)} %bitcast.106), calls=%async_computation.6 | async-start | bytes 2097152 | tf_op jit(solution)/shard_map/all_to_all | solution.py:111
  515.9 9.5 %copy.54 = bf16[2,1,2048,128]{3,0,2,1:T(2,128)(2,1)} copy(bf16[2,1,2048,128]{3,2,1,0:T(8,128)(2,1)S(1)} %copy-done.9) | data formatting | bytes 2097152 | tf_op jit(solution)/shard_map/while | solution.py:105
  535.4 10.6 %all-to-all-done.7 = bf16[2,2048,128]{2,0,1:T(2,128)(2,1)S(1)} async-done(((bf16[2,2048,128]{2,0,1:T(2,128)(2,1)}), bf16[2,2048,128]{2,0,1:T(2,128)(2,1)S(1)}, u32[]{:S(2)}, u32[]{:S(2)}) %all-to-all-start.7) | async-done | bytes 1048608 | tf_op jit(solution)/shard_map/all_to_all | solution.py:112
  (158 shorter events, 280.7 us)
Async XLA Ops:
  7.9 25.4 %all-to-all-start = ((bf16[32,2,8192]{2,1,0:T(2,128)(2,1)}), bf16[32,2,8192]{2,1,0:T(2,128)(2,1)S(1)}, u32[]{:S(2)}, u32[]{:S(2)}) async-start(bf16[32,2,8192]{2,1,0:T(2,128)(2,1)} %reshape.44), calls=%async_computation | async-start | bytes 2097152 | tf_op jit(solution)/shard_map/all_to_all | solution.py:58
  33.3 28.8 %copy-start.6 = (bf16[32,2,8192]{2,1,0:T(2,128)(2,1)}, bf16[32,2,8192]{2,1,0:T(2,128)(2,1)S(1)}, u32[]{:S(2)}) copy-start(bf16[32,2,8192]{2,1,0:T(2,128)(2,1)S(1)} %all-to-all-done) | copy-start | bytes 3145732
  33.3 36.2 %all-to-all-start.1 = ((bf16[32,2,8192]{2,1,0:T(2,128)(2,1)}), bf16[32,2,8192]{2,1,0:T(2,128)(2,1)}, u32[]{:S(2)}, u32[]{:S(2)}) async-start(bf16[32,2,8192]{2,1,0:T(2,128)(2,1)} %reshape.46), calls=%async_computation.1 | async-start | bytes 2097152 | tf_op jit(solution)/shard_map/all_to_all | solution.py:59
  39.2 16.8 %collective-permute-start = (bf16[1,64,4096]{2,1,0:T(8,128)(2,1)S(1)}, bf16[1,64,4096]{2,1,0:T(8,128)(2,1)S(1)}, u32[]{:S(2)}, u32[]{:S(2)}) collective-permute-start(bf16[1,64,4096]{2,1,0:T(8,128)(2,1)S(1)} %slice.12), channel_id=1, source_target_pairs={{0,32},{32,64},{64,96},{1,33},{33,65},{65,97},{2,34},{34,66},{66,9... | collective-permute-start | bytes 1572872 | tf_op jit(solution)/shard_map/ppermute | solution.py:14
  62.1 15.4 %copy-start.8 = (bf16[2,64,4096]{2,1,0:T(8,128)(2,1)S(1)}, bf16[2,64,4096]{2,1,0:T(8,128)(2,1)}, u32[]{:S(2)}) copy-start(bf16[2,64,4096]{2,1,0:T(8,128)(2,1)} %param.14) | copy-start | bytes 3145732
  69.5 36.3 %all-to-all-start.2 = ((bf16[32,2,12288]{2,1,0:T(2,128)(2,1)}), bf16[32,2,12288]{2,1,0:T(2,128)(2,1)S(1)}, u32[]{:S(2)}, u32[]{:S(2)}) async-start(bf16[32,2,12288]{2,1,0:T(2,128)(2,1)} %reshape.48), calls=%async_computation.2 | async-start | bytes 3145728 | tf_op jit(solution)/shard_map/all_to_all | solution.py:60
  77.6 14.9 %collective-permute-start.1 = (bf16[1,64,4096]{2,1,0:T(8,128)(2,1)S(1)}, bf16[1,64,4096]{2,1,0:T(8,128)(2,1)S(1)}, u32[]{:S(2)}, u32[]{:S(2)}) collective-permute-start(bf16[1,64,4096]{2,1,0:T(8,128)(2,1)S(1)} %slice.13), channel_id=1, source_target_pairs={{0,32},{32,64},{64,96},{1,33},{33,65},{65,97},{2,34},{34,66},{66,9... | collective-permute-start | bytes 1572872 | tf_op jit(solution)/shard_map/ppermute | solution.py:14
  105.8 31.7 %copy-start.1 = (bf16[32,2,12288]{2,1,0:T(2,128)(2,1)}, bf16[32,2,12288]{2,1,0:T(2,128)(2,1)S(1)}, u32[]{:S(2)}) copy-start(bf16[32,2,12288]{2,1,0:T(2,128)(2,1)S(1)} %all-to-all-done.2) | copy-start | bytes 4718596
  105.8 38.9 %all-to-all-start.3 = ((bf16[32,2,12288]{2,1,0:T(2,128)(2,1)}), bf16[32,2,12288]{2,1,0:T(2,128)(2,1)S(1)}, u32[]{:S(2)}, u32[]{:S(2)}) async-start(bf16[32,2,12288]{2,1,0:T(2,128)(2,1)} %reshape.50), calls=%async_computation.3 | async-start | bytes 3145728 | tf_op jit(solution)/shard_map/all_to_all | solution.py:62
  114.7 13.8 %collective-permute-start.2 = (bf16[1,64,4096]{2,1,0:T(8,128)(2,1)S(1)}, bf16[1,64,4096]{2,1,0:T(8,128)(2,1)S(1)}, u32[]{:S(2)}, u32[]{:S(2)}) collective-permute-start(bf16[1,64,4096]{2,1,0:T(8,128)(2,1)S(1)} %slice.14), channel_id=1, source_target_pairs={{0,32},{32,64},{64,96},{1,33},{33,65},{65,97},{2,34},{34,66},{66,9... | collective-permute-start | bytes 1572872 | tf_op jit(solution)/shard_map/ppermute | solution.py:14
  144.7 31.6 %copy-start.2 = (bf16[32,2,12288]{2,1,0:T(2,128)(2,1)}, bf16[32,2,12288]{2,1,0:T(2,128)(2,1)S(1)}, u32[]{:S(2)}) copy-start(bf16[32,2,12288]{2,1,0:T(2,128)(2,1)S(1)} %all-to-all-done.3) | copy-start | bytes 4718596
  144.7 38.9 %all-to-all-start.4 = ((bf16[32,2,12288]{2,1,0:T(2,128)(2,1)}), bf16[32,2,12288]{2,1,0:T(2,128)(2,1)S(1)}, u32[]{:S(2)}, u32[]{:S(2)}) async-start(bf16[32,2,12288]{2,1,0:T(2,128)(2,1)} %reshape.52), calls=%async_computation.4 | async-start | bytes 3145728 | tf_op jit(solution)/shard_map/all_to_all | solution.py:61
  153.6 13.8 %collective-permute-start.3 = (bf16[1,64,4096]{2,1,0:T(8,128)(2,1)S(1)}, bf16[1,64,4096]{2,1,0:T(8,128)(2,1)S(1)}, u32[]{:S(2)}, u32[]{:S(2)}) collective-permute-start(bf16[1,64,4096]{2,1,0:T(8,128)(2,1)S(1)} %slice.15), channel_id=1, source_target_pairs={{0,32},{32,64},{64,96},{1,33},{33,65},{65,97},{2,34},{34,66},{66,9... | collective-permute-start | bytes 1572872 | tf_op jit(solution)/shard_map/ppermute | solution.py:14
  176.4 15.4 %copy-start.7 = (bf16[32,2,8192]{2,1,0:T(2,128)(2,1)S(1)}, bf16[32,2,8192]{2,1,0:T(2,128)(2,1)}, u32[]{:S(2)}) copy-start(bf16[32,2,8192]{2,1,0:T(2,128)(2,1)} %copy-done.6) | copy-start | bytes 3145732
  183.7 8.0 %copy-start.4 = (bf16[32,2,12288]{2,1,0:T(2,128)(2,1)}, bf16[32,2,12288]{2,1,0:T(2,128)(2,1)S(1)}, u32[]{:S(2)}) copy-start(bf16[32,2,12288]{2,1,0:T(2,128)(2,1)S(1)} %all-to-all-done.4) | copy-start | bytes 4718596
  183.7 57.9 %all-to-all-start.5 = ((bf16[32,2,12288]{2,1,0:T(2,128)(2,1)}), bf16[32,2,12288]{2,1,0:T(2,128)(2,1)}, u32[]{:S(2)}, u32[]{:S(2)}) async-start(bf16[32,2,12288]{2,1,0:T(2,128)(2,1)} %reshape.54), calls=%async_computation.5 | async-start | bytes 3145728 | tf_op jit(solution)/shard_map/all_to_all | solution.py:63
  212.9 6.4 %copy-start.3 = (bf16[32,2,12288]{2,1,0:T(2,128)(2,1)S(1)}, bf16[32,2,12288]{2,1,0:T(2,128)(2,1)}, u32[]{:S(2)}) copy-start(bf16[32,2,12288]{2,1,0:T(2,128)(2,1)} %copy-done.2) | copy-start | bytes 4718596
  224.1 6.4 %copy-start.5 = (bf16[32,2,12288]{2,1,0:T(2,128)(2,1)S(1)}, bf16[32,2,12288]{2,1,0:T(2,128)(2,1)}, u32[]{:S(2)}) copy-start(bf16[32,2,12288]{2,1,0:T(2,128)(2,1)} %copy-done.4) | copy-start | bytes 4718596
  287.4 4.9 copy-start
  314.0 4.9 copy-start
  340.6 4.9 copy-start
  367.2 4.9 copy-start
  411.5 4.9 copy-start
  438.1 4.9 copy-start
  464.7 4.9 copy-start
  491.3 4.9 copy-start
  503.8 12.0 %copy-start.9 = (bf16[2,1,2048,128]{3,2,1,0:T(8,128)(2,1)S(1)}, bf16[2,1,2048,128]{3,2,1,0:T(8,128)(2,1)}, u32[]{:S(2)}) copy-start(bf16[2,1,2048,128]{3,2,1,0:T(8,128)(2,1)} %get-tuple-element.224) | copy-start | bytes 3145732
  507.6 20.9 %all-to-all-start.6 = ((bf16[2,2048,128]{2,0,1:T(2,128)(2,1)}), bf16[2,2048,128]{2,0,1:T(2,128)(2,1)S(1)}, u32[]{:S(2)}, u32[]{:S(2)}) async-start(bf16[2,2048,128]{2,0,1:T(2,128)(2,1)} %bitcast.106), calls=%async_computation.6 | async-start | bytes 2097152 | tf_op jit(solution)/shard_map/all_to_all | solution.py:111
  528.5 17.5 %all-to-all-start.7 = ((bf16[2,2048,128]{2,0,1:T(2,128)(2,1)}), bf16[2,2048,128]{2,0,1:T(2,128)(2,1)S(1)}, u32[]{:S(2)}, u32[]{:S(2)}) async-start(bf16[2,2048,128]{2,0,1:T(2,128)(2,1)} %bitcast.105), calls=%async_computation.7 | async-start | bytes 2097152 | tf_op jit(solution)/shard_map/all_to_all | solution.py:112
where the time goes:
time: 552 us; the launch traced here: 548 us
  matrix products  195 us (35%)
  local copies, waits for them, and re-layouts  171 us (31%)
  waiting for transfers between devices  74.6 us (14%)
  starting transfers between devices  66.2 us (12%)
  other arithmetic  29.7 us (5%)
  loops' own time  10.5 us (2%)
    dot_general x24, matrix products, contract(): lax.dot_general(left, right, (((1,), (1,)), ((), ())), preferred_element_...  125 us
    unnamed x32, local copies, waits for them, and re-layouts  73.8 us
    ppermute x4, waiting for transfers between devices, from_behind(): return lax.ppermute(block, axis, route)  51.6 us
    dot_general x8, matrix products, attend_block(): jnp.dot(probs_dot_low, values, preferred_element_type=jnp.float32)  39.1 us
    concatenate x4, local copies, waits for them, and re-layouts, per_device(): jnp.concatenate([first, rest], axis=0)  22.3 us
    reduce_sum x8, other arithmetic, attend_block(): probs = weights / jnp.sum(weights, axis=1, keepdims=True)  17.3 us
    dot_general x8, matrix products, attend_block(): jnp.dot(probs_low, values_dot, preferred_element_type=jnp.float32)  15.4 us
    dot_general x8, matrix products, attend_block(): output = jnp.dot(probs_low, values, preferred_element_type=jnp.float32)  15.3 us
  transfers between devices with their start and end apart: 12, of which 7 were waited for; matrix products, arithmetic and copies ran while one was open for 24% of the time, Pallas kernels for 0%

commit v1 on v0

v1 whole, which is shorter than its diff:
```python
import functools
import math

import jax
import jax.numpy as jnp
from jax import lax
from jax.experimental import pallas as pl
from jax.experimental.pallas import tpu as pltpu
from jax.sharding import PartitionSpec as P

HD = 128
FACTOR = 1.0 / math.sqrt(HD)
LOG2_FACTOR = FACTOR * math.log2(math.e)
MESH = pl.DeviceIdType.MESH
COMPUTE = True
OUTPUTS = True
QS = True
PIECE = 16
ROWS = 256


def contract(left, right):
    return lax.dot_general(
        left, right, (((1,), (1,)), ((), ())), preferred_element_type=jnp.float32
    )


def product(left, right):
    return jnp.dot(left, right, preferred_element_type=jnp.float32)


def frame_part(query, query_dot, key, key_dot, value, value_dot):
    scores = contract(query, key)
    scores_dot = contract(
        jnp.concatenate([query_dot, query], axis=1), jnp.concatenate([key, key_dot], axis=1)
    )
    top = jnp.max(scores, axis=1, keepdims=True)
    weights = jnp.exp2((scores - top) * LOG2_FACTOR)
    total = jnp.sum(weights, axis=1, keepdims=True)
    center = jnp.sum(weights * scores_dot, axis=1, keepdims=True) / total
    weights_dot = (weights * (scores_dot - center)).astype(jnp.bfloat16)
    both = product(weights.astype(jnp.bfloat16), jnp.concatenate([value, value_dot], axis=1))
    return top, total, center, both[:, :HD], both[:, HD:], product(weights_dot, value)


def combine(parts):
    top = functools.reduce(jnp.maximum, [part[0] for part in parts])
    shares = [jnp.exp2((part[0] - top) * LOG2_FACTOR) for part in parts]
    inverse = 1.0 / sum(share * part[1] for share, part in zip(shares, parts))
    shares = [share * inverse for share in shares]
    center = sum(share * part[1] * part[2] for share, part in zip(shares, parts))
    output = sum(share * part[3] for share, part in zip(shares, parts))
    output_dot = sum(
        share * ((part[5] + (part[2] - center) * part[3]) * FACTOR + part[4])
        for share, part in zip(shares, parts)
    )
    return output.astype(jnp.bfloat16), output_dot.astype(jnp.bfloat16)


def kernel(groups, devices, flip, *refs):
    ins, outs, refs = refs[:6], refs[6:8], refs[8:]
    kv_bufs, q_bufs, o_bufs, refs = refs[:4], refs[4:6], refs[6:8], refs[8:]
    kv_send, kv_recv, halo_send, halo_recv, q_send, q_recv, o_send, o_recv = refs
    query, key_in, value, query_dot, key_dot, value_dot = ins
    kvs = (key_in, key_dot, value, value_dot)
    qs = (query, query_dot)
    group, me = lax.axis_index("tm"), lax.axis_index("head")
    tokens = query.shape[1]
    pieces = tokens // PIECE
    first = group == 0
    high = group // 2
    my_head = me ^ (high * flip)
    my_columns = pl.ds(pl.multiple_of(my_head * HD, HD), HD)
    odd = lax.rem(group, 2)
    next_place = (lax.rem(group + 1, groups), me ^ (odd * flip))
    prior_place = (lax.rem(group + groups - 1, groups), me ^ ((1 - odd) * flip))

    barrier = pltpu.get_barrier_semaphore()

    def greet(step, carry):
        peer = lax.rem(me + step, devices)
        pl.semaphore_signal(barrier, inc=1, device_id=(group, peer), device_id_type=MESH)
        return carry

    lax.fori_loop(1, devices, greet, 0)

    for place in (prior_place, next_place):
        pl.semaphore_signal(barrier, inc=1, device_id=place, device_id_type=MESH)
    pl.semaphore_wait(barrier, devices + 1)

    def rows_of(place, size):
        return pl.ds(pl.multiple_of(place * size, size), size)

    def head_columns(peer):
        return pl.ds(pl.multiple_of((peer ^ (high * flip)) * HD, HD), HD)

    def send_keys(frame):
        def one(peer, remote):
            for i, (source, buf) in enumerate(zip(kvs, kv_bufs)):
                src = source.at[frame, :, head_columns(peer)]
                dst = buf.at[frame + 1, rows_of(me, tokens), :]
                if remote:
                    pltpu.make_async_remote_copy(
                        src, dst, kv_send.at[frame, i], kv_recv.at[frame, i],
                        device_id=(group, peer), device_id_type=MESH,
                    ).start()
                else:
                    pltpu.make_async_copy(src, dst, kv_recv.at[frame, i]).start()

        def loop(step, carry):
            one(lax.rem(me + step, devices), True)
            return carry

        lax.fori_loop(1, devices, loop, 0)
        one(me, False)

    def send_queries(frame, piece):
        slot = frame * pieces + piece

        def one(peer, remote):
            for i, (source, buf) in enumerate(zip(qs, q_bufs)):
                src = source.at[frame, pl.ds(piece * PIECE, PIECE), head_columns(peer)]
                dst = buf.at[slot, rows_of(me, PIECE), :]
                if remote:
                    pltpu.make_async_remote_copy(
                        src, dst, q_send.at[slot, i], q_recv.at[slot, i],
                        device_id=(group, peer), device_id_type=MESH,
                    ).start()
                else:
                    pltpu.make_async_copy(src, dst, q_recv.at[slot, i]).start()

        def loop(step, carry):
            one(lax.rem(me + step, devices), True)
            return carry

        lax.fori_loop(1, devices, loop, 0)
        one(me, False)

    def send_outputs(frame, piece):
        slot = frame * pieces + piece

        def one(peer, remote):
            for i, (buf, target) in enumerate(zip(o_bufs, outs)):
                src = buf.at[slot, rows_of(peer, PIECE), :]
                dst = target.at[frame, pl.ds(piece * PIECE, PIECE), my_columns]
                if remote:
                    pltpu.make_async_remote_copy(
                        src, dst, o_send.at[i], o_recv.at[i],
                        device_id=(group, peer), device_id_type=MESH,
                    ).start()
                else:
                    pltpu.make_async_copy(src, dst, o_recv.at[i]).start()

        def loop(step, carry):
            one(lax.rem(me + step, devices), True)
            return carry

        lax.fori_loop(1, devices, loop, 0)
        one(me, False)

    def await_bytes(ref, semaphore):
        pltpu.make_async_copy(ref, ref, semaphore).wait()

    blocks = [(frame, piece) for frame in (1, 0) for piece in range(pieces)]
    send_keys(1)
    send_keys(0)
    if QS:
        for frame, piece in blocks:
            send_queries(frame, piece)

    def halo(buf, i):
        return pltpu.make_async_remote_copy(
            buf.at[2], buf.at[0], halo_send.at[i], halo_recv.at[i],
            device_id=next_place, device_id_type=MESH,
        )

    for i, buf in enumerate(kv_bufs):
        await_bytes(buf.at[2], kv_recv.at[1, i])

    for i, buf in enumerate(kv_bufs):
        halo(buf, i).start()

    for i, buf in enumerate(kv_bufs):
        await_bytes(buf.at[1], kv_recv.at[0, i])

    def block_compute(frame, slot):
        steps = q_bufs[0].shape[1] // ROWS

        def step(index, carry):
            rows = rows_of(index, ROWS)
            q, qd = (buf[slot, rows, :] for buf in q_bufs)
            parts = []
            for key_slot in (frame, frame + 1):
                keys = [buf[key_slot] for buf in kv_bufs]
                parts.append(frame_part(q, qd, *keys))
            if frame == 0:
                top, *rest = parts[0]
                parts[0] = (jnp.where(first, -1e30, top), jnp.where(first, 0.0, rest[0]), *rest[1:])
            output, output_dot = combine(parts)
            o_bufs[0][slot, rows, :] = output
            o_bufs[1][slot, rows, :] = output_dot
            return carry

        lax.fori_loop(0, steps, step, 0)

    for frame in (1, 0):
        if frame == 0:
            for i, buf in enumerate(kv_bufs):
                await_bytes(buf.at[0], halo_recv.at[i])
        for piece in range(pieces):
            slot = frame * pieces + piece
            if QS:
                for i, buf in enumerate(q_bufs):
                    await_bytes(buf.at[slot], q_recv.at[slot, i])
            if COMPUTE:
                block_compute(frame, slot)
            if OUTPUTS:
                send_outputs(frame, piece)

    for i, buf in enumerate(kv_bufs):
        await_bytes(buf.at[2], halo_send.at[i])

    share = (devices - 1) * tokens
    for frame in (0, 1):
        for i, buf in enumerate(kv_bufs):
            await_bytes(buf.at[frame + 1, pl.ds(0, share)], kv_send.at[frame, i])
        for piece in range(pieces):
            if QS:
                for i, buf in enumerate(q_bufs):
                    slot = frame * pieces + piece
                    await_bytes(buf.at[slot, pl.ds(0, (devices - 1) * PIECE)], q_send.at[slot, i])
    if OUTPUTS:
        for i, (buf, target) in enumerate(zip(o_bufs, outs)):
            await_bytes(buf.at[:, pl.ds(0, (devices - 1) * PIECE)], o_send.at[i])
            await_bytes(target, o_recv.at[i])


def per_device(*args):
    groups, devices = lax.axis_size("tm"), lax.axis_size("head")
    frames, tokens, model = args[0].shape
    width = tokens * devices
    slots = frames * tokens // PIECE
    bf16 = jnp.bfloat16
    kv = pltpu.VMEM((frames + 1, width, HD), bf16)
    q = pltpu.VMEM((slots, devices * PIECE, HD), bf16)
    dma = pltpu.SemaphoreType.DMA
    return pl.pallas_call(
        functools.partial(kernel, groups, devices, 4),
        out_shape=[jax.ShapeDtypeStruct((frames, tokens, model), bf16)] * 2,
        in_specs=[pl.BlockSpec(memory_space=pl.ANY)] * 6,
        out_specs=[pl.BlockSpec(memory_space=pl.ANY)] * 2,
        scratch_shapes=[kv] * 4 + [q] * 4
        + [dma((2, 4)), dma((2, 4)), dma((4,)), dma((4,)), dma((slots, 2)), dma((slots, 2)), dma((2,)), dma((2,))],
        compiler_params=pltpu.CompilerParams(
            collective_id=0, has_side_effects=True, vmem_limit_bytes=56 * 1024 * 1024
        ),
    )(*args)


def solution(mesh):
    spec = P("tm", "head", None)
    return jax.shard_map(
        per_device, mesh=mesh, in_specs=(spec,) * 6, out_specs=(spec, spec), check_vma=False
    )
```

time: 552 us -> 155 us (0.28)
  matrix products: 195 us -> 0 us
  local copies, waits for them, and re-layouts: 171 us -> 3.35 us
  Pallas kernels: 0 us -> 148 us
  waiting for transfers between devices: 74.6 us -> 0 us
  starting transfers between devices: 66.2 us -> 0 us
  other arithmetic: 29.7 us -> 0 us
  loops' own time: 10.5 us -> 0 us
    dot_general x48 -> x0, matrix products: 195 us -> none  [the longest x24 125 us: contract(): lax.dot_general(left, right, (((1,), (1,)), ((), ())), preferred_element_...]
    pallas_call x0 -> x1, Pallas kernels: none -> 148 us  [per_device(): pl.pallas_call(functools.partial(kernel, groups, devices, 4), out_shape=[...]
    unnamed x32 -> x4, local copies, waits for them, and re-layouts: 73.8 us -> 3.35 us
    all_to_all x8 -> x0, starting transfers between devices: 58.5 us -> none  [the longest x1 8.88 us: to_heads(): lax.all_to_all(query, 'head', split_axis=2, concat_axis=1, tiled=True)]
    ppermute x4 -> x0, waiting for transfers between devices: 51.6 us -> none  [from_behind(): return lax.ppermute(block, axis, route)]
    all_to_all x10 -> x0, local copies, waits for them, and re-layouts: 37.1 us -> none  [the longest x1 6.44 us: to_heads(): lax.all_to_all(keys_dot, 'head', split_axis=2, concat_axis=1, tiled=True)]
    all_to_all x8 -> x0, waiting for transfers between devices: 23 us -> none  [the longest x1 10.6 us: per_device(): lax.all_to_all(merge(output_dot), 'head', split_axis=1, concat_axis=2, ti...]
    concatenate x4 -> x0, local copies, waits for them, and re-layouts: 22.3 us -> none  [per_device(): jnp.concatenate([first, rest], axis=0)]
  transfers between devices with their start and end apart: 12 -> 0, of which waited for: 7 -> 0; matrix products, arithmetic and copies ran while one was open for 24% -> 0% of each run, Pallas kernels for 0% -> 0%
where the time goes in v1:
time: 155 us; the launch traced here: 152 us
  Pallas kernels  148 us (95%)
  local copies, waits for them, and re-layouts  3.35 us (2%)
    pallas_call x1, Pallas kernels, per_device(): pl.pallas_call(functools.partial(kernel, groups, devices, 4), out_shape=[...  148 us
    unnamed x4, local copies, waits for them, and re-layouts  3.35 us

profile of v1, /device:TPU:16, one launch (start us, length us, event | category | flops | bytes accessed | tf_op | source)
XLA Modules:
  0.0 151.6 jit_solution(10276964170624567775)
XLA Ops:
  0.6 147.6 %shard_map.77 = (bf16[2,64,4096]{2,1,0:T(8,128)(2,1)}, bf16[2,64,4096]{2,1,0:T(8,128)(2,1)}) custom-call(bf16[2,64,4096]{2,1,0:T(8,128)(2,1)} %refs_0_.1, bf16[2,64,4096]{2,1,0:T(8,128)(2,1)} %refs_1_.1, bf16[2,64,4096]{2,1,0:T(8,128)(2,1)} %refs_2_.1, bf16[2,64,4096]{2,1,0:T(8,128)(2,1)} %refs_3_.1, bf16[2,64,4096]{2,1,0:T(8,128)(2,1)} %refs_4_.1, ...), custom_call_target="tpu_custom_call" | custom-call | tf_op jit(solution)/shard_map/pallas_call | solution.py:247
  148.2 0.0 copy-start
  148.2 2.4 %copy.10 = bf16[2,64,4096]{2,1,0:T(8,128)(2,1)} copy(bf16[2,64,4096]{2,1,0:T(8,128)(2,1)} %get-tuple-element.4) | data formatting | bytes 2097152
  150.6 0.0 copy-done
  150.6 1.0 copy.11
Async XLA Ops:
  148.2 2.4 %copy-start = (bf16[2,64,4096]{2,1,0:T(8,128)(2,1)S(1)}, bf16[2,64,4096]{2,1,0:T(8,128)(2,1)}, u32[]{:S(2)}) copy-start(bf16[2,64,4096]{2,1,0:T(8,128)(2,1)} %get-tuple-element.5) | copy-start | bytes 3145732

commit v2 on v0

v2 whole, which is shorter than its diff:
```python
import functools
import math

import jax
import jax.numpy as jnp
from jax import lax
from jax.experimental import pallas as pl
from jax.experimental.pallas import tpu as pltpu
from jax.sharding import PartitionSpec as P

HD = 128
FACTOR = 1.0 / math.sqrt(HD)
LOG2_FACTOR = FACTOR * math.log2(math.e)
MESH = pl.DeviceIdType.MESH
STRIDE = 13
OWNERS = 4


def contract(left, right):
    return lax.dot_general(
        left, right, (((1,), (1,)), ((), ())), preferred_element_type=jnp.float32
    )


def product(left, right):
    return jnp.dot(left, right, preferred_element_type=jnp.float32)


def attend(query, query_dot, key, key_dot, value, value_dot):
    scores = contract(query, key)
    scores_dot = contract(
        jnp.concatenate([query_dot, query], axis=1), jnp.concatenate([key, key_dot], axis=1)
    )
    top = jnp.max(scores, axis=1, keepdims=True)
    weights = jnp.exp2((scores - top) * LOG2_FACTOR)
    total = jnp.sum(weights, axis=1, keepdims=True)
    center = jnp.sum(weights * scores_dot, axis=1, keepdims=True) / total
    weights_dot = (weights * (scores_dot - center)).astype(jnp.bfloat16)
    both = product(weights.astype(jnp.bfloat16), jnp.concatenate([value, value_dot], axis=1))
    return top, total, center, both[:, :HD], both[:, HD:], product(weights_dot, value)


def join(one, two):
    top = jnp.maximum(one[0], two[0])
    parts = [(jnp.exp2((part[0] - top) * LOG2_FACTOR), *part[1:]) for part in (one, two)]
    total = sum(share * part for share, part, *_ in parts)
    center = sum(share * part * mean for share, part, mean, *_ in parts) / total
    output = sum(share * out for share, _, _, out, _, _ in parts)
    output_dot = sum(share * dot for share, _, _, _, dot, _ in parts)
    spread = sum(
        share * (dot + (mean - center) * out) for share, _, mean, out, _, dot in parts
    )
    return top, total, center, output, output_dot, spread


def finish(part):
    _, total, _, output, output_dot, spread = part
    inverse = 1.0 / total
    return (
        (output * inverse).astype(jnp.bfloat16),
        ((spread * FACTOR + output_dot) * inverse).astype(jnp.bfloat16),
    )


def kernel(groups, devices, *refs):
    ins, outs, refs = refs[:6], refs[6:8], refs[8:]
    kv_bufs, q_bufs, o_bufs, refs = refs[:4], refs[4:6], refs[6:8], refs[8:]
    stats, sums, kv_send, kv_recv, halo_send, halo_recv, q_send, q_recv, o_send, o_recv = refs
    query, key_in, value, query_dot, key_dot, value_dot = ins
    kvs = (key_in, key_dot, value, value_dot)
    qs = (query, query_dot)
    group, me = lax.axis_index("tm"), lax.axis_index("head")
    tokens = query.shape[1]
    half = tokens // 2
    width = tokens * devices
    rows = OWNERS * tokens
    high, odd = group // 2, lax.rem(group, 2)
    next_place = (lax.rem(group + 1, groups), me ^ (odd * 4))
    prior_place = (lax.rem(group + groups - 1, groups), me ^ ((1 - odd) * 4))

    def head_columns(device):
        return pl.ds(pl.multiple_of((device ^ (high * 4)) * HD, HD), HD)

    def rows_of(place, size):
        return pl.ds(pl.multiple_of(place * size, size), size)

    def partner(step):
        offset = lax.rem(step * STRIDE, devices)
        x = lax.rem(me // 8 + offset // 8, 4)
        y = lax.rem(me // 4 + offset // 4, 2)
        z = lax.rem(me + offset, 4)
        return x * 8 + y * 4 + z

    def send_all(source, dest, send, recv):
        def step(index, carry):
            peer = partner(index)
            pltpu.make_async_remote_copy(
                source(peer), dest, send, recv, device_id=(group, peer), device_id_type=MESH
            ).start()
            return carry

        lax.fori_loop(1, devices, step, 0)
        pltpu.make_async_copy(source(me), dest, recv).start()

    def send_keys(frame, part):
        for i, (source, buf) in enumerate(zip(kvs, kv_bufs)):
            send_all(
                lambda peer: source.at[frame, pl.ds(part * half, half), head_columns(peer)],
                buf.at[frame + 1, part, rows_of(me, half)],
                kv_send.at[frame, part, i],
                kv_recv.at[frame, part, i],
            )

    def send_queries(frame):
        for i, (source, buf) in enumerate(zip(qs, q_bufs)):
            send_all(
                lambda peer: source.at[frame, :, head_columns(peer)],
                buf.at[frame, rows_of(me, tokens)],
                q_send.at[frame, i],
                q_recv.at[frame, i],
            )

    def await_bytes(ref, semaphore):
        pltpu.make_async_copy(ref, ref, semaphore).wait()

    def await_keys(frame, part):
        for i, buf in enumerate(kv_bufs):
            await_bytes(buf.at[frame + 1, part], kv_recv.at[frame, part, i])

    def await_queries(frame):
        for i, buf in enumerate(q_bufs):
            await_bytes(buf.at[frame], q_recv.at[frame, i])

    def halo(i, buf):
        return pltpu.make_async_remote_copy(
            buf.at[2], buf.at[0], halo_send.at[i], halo_recv.at[i],
            device_id=next_place, device_id_type=MESH,
        )

    def block_of(index):
        x = lax.rem(me // 8 + (index + 1) // 2, 4)
        y = lax.rem(me // 4 + index + 1, 2)
        return x * 2 + y

    def load_queries(frame, block):
        return [buf[frame, rows_of(block, rows)] for buf in q_bufs]

    def load_keys(slot, part=None):
        if part is not None:
            return [buf[slot, part] for buf in kv_bufs]
        return [buf[slot].reshape(width, HD) for buf in kv_bufs]

    def load_state(block):
        place = rows_of(block, rows)
        return [stats[i, place] for i in range(3)] + [sums[i, place] for i in range(3)]

    def store_state(block, state):
        place = rows_of(block, rows)
        for i in range(3):
            stats[i, place] = state[i]
            sums[i, place] = state[i + 3]

    def send_outputs(frame, block, results):
        for buf, result in zip(o_bufs, results):
            buf[frame, rows_of(block, rows)] = result
        for j in range(OWNERS):
            owner = block * OWNERS + lax.rem(me + j, OWNERS)
            for i, (buf, target) in enumerate(zip(o_bufs, outs)):
                source = buf.at[frame, rows_of(owner, tokens)]
                dest = target.at[frame, :, head_columns(me)]

                def push():
                    pltpu.make_async_remote_copy(
                        source, dest, o_send.at[i], o_recv.at[i],
                        device_id=(group, owner), device_id_type=MESH,
                    ).start()

                if j:
                    push()
                else:
                    own = owner == me
                    pl.when(jnp.logical_not(own))(push)

                    @pl.when(own)
                    def _():
                        pltpu.make_async_copy(source, dest, o_recv.at[i]).start()

    def each_block(body):
        def step(index, carry):
            body(block_of(index))
            return carry

        lax.fori_loop(0, width // rows, step, 0)

    barrier = pltpu.get_barrier_semaphore()

    def greet(step, carry):
        peer = lax.rem(me + step, devices)
        pl.semaphore_signal(barrier, inc=1, device_id=(group, peer), device_id_type=MESH)
        return carry

    lax.fori_loop(1, devices, greet, 0)
    for place in (prior_place, next_place):
        pl.semaphore_signal(barrier, inc=1, device_id=place, device_id_type=MESH)
    pl.semaphore_wait(barrier, devices + 1)

    send_keys(1, 0)
    send_keys(1, 1)
    send_queries(1)
    await_keys(1, 0)
    await_keys(1, 1)
    for i, buf in enumerate(kv_bufs):
        halo(i, buf).start()
    send_keys(0, 0)
    send_keys(0, 1)
    send_queries(0)

    await_queries(1)

    @each_block
    def _(block):
        store_state(block, attend(*load_queries(1, block), *load_keys(2)))

    await_keys(0, 0)

    @each_block
    def _(block):
        part = attend(*load_queries(1, block), *load_keys(1, 0))
        store_state(block, join(load_state(block), part))

    await_keys(0, 1)

    @each_block
    def _(block):
        part = attend(*load_queries(1, block), *load_keys(1, 1))
        send_outputs(1, block, finish(join(load_state(block), part)))

    await_queries(0)
    for i, buf in enumerate(kv_bufs):
        await_bytes(buf.at[0], halo_recv.at[i])

    @each_block
    def _(block):
        queries = load_queries(0, block)
        own = attend(*queries, *load_keys(1))
        prior = attend(*queries, *load_keys(0))
        first = group == 0
        prior = (jnp.where(first, -1e30, prior[0]), jnp.where(first, 0.0, prior[1]), *prior[2:])
        send_outputs(0, block, finish(join(prior, own)))

    for i, buf in enumerate(kv_bufs):
        await_bytes(buf.at[2], halo_send.at[i])
        for frame in (0, 1):
            for part in (0, 1):
                sent = buf.at[frame + 1, part, pl.ds(0, (devices - 1) * half)]
                await_bytes(sent, kv_send.at[frame, part, i])
    for i in (0, 1):
        for frame in (0, 1):
            sent = q_bufs[i].at[frame, pl.ds(0, (devices - 1) * tokens)]
            await_bytes(sent, q_send.at[frame, i])
        await_bytes(o_bufs[i].at[:, pl.ds(0, (devices - 1) * tokens)], o_send.at[i])
        await_bytes(outs[i], o_recv.at[i])


def per_device(*args):
    groups, devices = lax.axis_size("tm"), lax.axis_size("head")
    frames, tokens, model = args[0].shape
    width = tokens * devices
    bf16 = jnp.bfloat16
    kv = pltpu.VMEM((frames + 1, 2, width // 2, HD), bf16)
    q = pltpu.VMEM((frames, width, HD), bf16)
    stats = pltpu.VMEM((3, width, 1), jnp.float32)
    sums = pltpu.VMEM((3, width, HD), jnp.float32)
    dma = pltpu.SemaphoreType.DMA
    sems = [dma(dims) for dims in ((2, 2, 4), (2, 2, 4), (4,), (4,), (2, 2), (2, 2), (2,), (2,))]
    return pl.pallas_call(
        functools.partial(kernel, groups, devices),
        out_shape=[jax.ShapeDtypeStruct((frames, tokens, model), bf16)] * 2,
        in_specs=[pl.BlockSpec(memory_space=pl.ANY)] * 6,
        out_specs=[pl.BlockSpec(memory_space=pl.ANY)] * 2,
        scratch_shapes=[kv] * 4 + [q] * 4 + [stats, sums] + sems,
        compiler_params=pltpu.CompilerParams(
            collective_id=0, has_side_effects=True, vmem_limit_bytes=56 * 1024 * 1024
        ),
    )(*args)


def solution(mesh):
    spec = P("tm", "head", None)
    return jax.shard_map(
        per_device, mesh=mesh, in_specs=(spec,) * 6, out_specs=(spec, spec), check_vma=False
    )
```

time: 552 us -> 117 us (0.21)
  the two profiles are of different devices: /device:TPU:16 before, /device:TPU:6 now
where the time goes in v2:
time: 117 us
  Pallas kernels  113 us (97%)
  local copies, waits for them, and re-layouts  3.35 us (3%)
    pallas_call x1, Pallas kernels, per_device(): pl.pallas_call(functools.partial(kernel, groups, devices), out_shape=[jax...  113 us
    unnamed x4, local copies, waits for them, and re-layouts  3.35 us

profile of v2, /device:TPU:6, one launch (start us, length us, event | category | flops | bytes accessed | tf_op | source)
XLA Modules:
  0.0 116.9 jit_solution(15487099634482929263)
XLA Ops:
  0.6 112.9 %shard_map.77 = (bf16[2,64,4096]{2,1,0:T(8,128)(2,1)}, bf16[2,64,4096]{2,1,0:T(8,128)(2,1)}) custom-call(bf16[2,64,4096]{2,1,0:T(8,128)(2,1)} %refs_0_.1, bf16[2,64,4096]{2,1,0:T(8,128)(2,1)} %refs_1_.1, bf16[2,64,4096]{2,1,0:T(8,128)(2,1)} %refs_2_.1, bf16[2,64,4096]{2,1,0:T(8,128)(2,1)} %refs_3_.1, bf16[2,64,4096]{2,1,0:T(8,128)(2,1)} %refs_4_.1, ...), custom_call_target="tpu_custom_call" | custom-call | tf_op jit(solution)/shard_map/pallas_call | solution.py:276
  113.5 0.0 copy-start
  113.5 2.4 %copy.10 = bf16[2,64,4096]{2,1,0:T(8,128)(2,1)} copy(bf16[2,64,4096]{2,1,0:T(8,128)(2,1)} %get-tuple-element.4) | data formatting | bytes 2097152
  115.9 0.0 copy-done
  115.9 1.0 copy.11
Async XLA Ops:
  113.5 2.4 %copy-start = (bf16[2,64,4096]{2,1,0:T(8,128)(2,1)S(1)}, bf16[2,64,4096]{2,1,0:T(8,128)(2,1)}, u32[]{:S(2)}) copy-start(bf16[2,64,4096]{2,1,0:T(8,128)(2,1)} %get-tuple-element.5) | copy-start | bytes 3145732

commit v3 on v2

--- a/solution.py
+++ b/solution.py
@@ -13,7 +13,7 @@
 LOG2_FACTOR = FACTOR * math.log2(math.e)
 MESH = pl.DeviceIdType.MESH
 STRIDE = 13
-OWNERS = 4
+OWNERS = 8
 
 
 def contract(left, right):
@@ -138,9 +138,7 @@
         )
 
     def block_of(index):
-        x = lax.rem(me // 8 + (index + 1) // 2, 4)
-        y = lax.rem(me // 4 + index + 1, 2)
-        return x * 2 + y
+        return lax.rem(me // OWNERS + index + 1, devices // OWNERS)
 
     def load_queries(frame, block):
         return [buf[frame, rows_of(block, rows)] for buf in q_bufs]
@@ -150,15 +148,15 @@
             return [buf[slot, part] for buf in kv_bufs]
         return [buf[slot].reshape(width, HD) for buf in kv_bufs]
 
-    def load_state(block):
+    def load_state(frame, block):
         place = rows_of(block, rows)
-        return [stats[i, place] for i in range(3)] + [sums[i, place] for i in range(3)]
-
-    def store_state(block, state):
+        return [stats[frame, i, place] for i in range(3)] + [sums[frame, i, place] for i in range(3)]
+
+    def store_state(frame, block, state):
         place = rows_of(block, rows)
         for i in range(3):
-            stats[i, place] = state[i]
-            sums[i, place] = state[i + 3]
+            stats[frame, i, place] = state[i]
+            sums[frame, i, place] = state[i + 3]
 
     def send_outputs(frame, block, results):
         for buf, result in zip(o_bufs, results):
@@ -212,28 +210,20 @@
     for i, buf in enumerate(kv_bufs):
         halo(i, buf).start()
     send_keys(0, 0)
+    send_queries(0)
     send_keys(0, 1)
-    send_queries(0)
-
     await_queries(1)
 
     @each_block
     def _(block):
-        store_state(block, attend(*load_queries(1, block), *load_keys(2)))
+        store_state(1, block, attend(*load_queries(1, block), *load_keys(2)))
 
     await_keys(0, 0)
 
     @each_block
     def _(block):
         part = attend(*load_queries(1, block), *load_keys(1, 0))
-        store_state(block, join(load_state(block), part))
-
-    await_keys(0, 1)
-
-    @each_block
-    def _(block):
-        part = attend(*load_queries(1, block), *load_keys(1, 1))
-        send_outputs(1, block, finish(join(load_state(block), part)))
+        store_state(1, block, join(load_state(1, block), part))
 
     await_queries(0)
     for i, buf in enumerate(kv_bufs):
@@ -241,12 +231,22 @@
 
     @each_block
     def _(block):
-        queries = load_queries(0, block)
-        own = attend(*queries, *load_keys(1))
-        prior = attend(*queries, *load_keys(0))
+        top, total, *rest = attend(*load_queries(0, block), *load_keys(0))
         first = group == 0
-        prior = (jnp.where(first, -1e30, prior[0]), jnp.where(first, 0.0, prior[1]), *prior[2:])
-        send_outputs(0, block, finish(join(prior, own)))
+        top, total = jnp.where(first, -1e30, top), jnp.where(first, 0.0, total)
+        store_state(0, block, (top, total, *rest))
+
+    await_keys(0, 1)
+
+    @each_block
+    def _(block):
+        part = attend(*load_queries(1, block), *load_keys(1, 1))
+        send_outputs(1, block, finish(join(load_state(1, block), part)))
+
+    @each_block
+    def _(block):
+        part = attend(*load_queries(0, block), *load_keys(1))
+        send_outputs(0, block, finish(join(load_state(0, block), part)))
 
     for i, buf in enumerate(kv_bufs):
         await_bytes(buf.at[2], halo_send.at[i])
@@ -269,15 +269,15 @@
     bf16 = jnp.bfloat16
     kv = pltpu.VMEM((frames + 1, 2, width // 2, HD), bf16)
     q = pltpu.VMEM((frames, width, HD), bf16)
-    stats = pltpu.VMEM((3, width, 1), jnp.float32)
-    sums = pltpu.VMEM((3, width, HD), jnp.float32)
+    stats = pltpu.VMEM((frames, 3, width, 1), jnp.float32)
+    sums = pltpu.VMEM((frames, 3, width, HD), jnp.float32)
     dma = pltpu.SemaphoreType.DMA
     sems = [dma(dims) for dims in ((2, 2, 4), (2, 2, 4), (4,), (4,), (2, 2), (2, 2), (2,), (2,))]
     return pl.pallas_call(
         functools.partial(kernel, groups, devices),
-        out_shape=[jax.ShapeDtypeStruct((frames, tokens, model), bf16)] * 2,
+        out_shape=[pltpu.VMEM((frames, tokens, model), bf16)] * 2,
         in_specs=[pl.BlockSpec(memory_space=pl.ANY)] * 6,
-        out_specs=[pl.BlockSpec(memory_space=pl.ANY)] * 2,
+        out_specs=[pl.BlockSpec(memory_space=pltpu.VMEM)] * 2,
         scratch_shapes=[kv] * 4 + [q] * 4 + [stats, sums] + sems,
         compiler_params=pltpu.CompilerParams(
             collective_id=0, has_side_effects=True, vmem_limit_bytes=56 * 1024 * 1024

time: 117 us -> 114 us (0.974)
  the two profiles are of different devices: /device:TPU:6 before, /device:TPU:16 now
where the time goes in v3:
time: 114 us; the launch traced here: 112 us
  Pallas kernels  109 us (96%)
  local copies, waits for them, and re-layouts  1.94 us (2%)
    pallas_call x1, Pallas kernels, per_device(): pl.pallas_call(functools.partial(kernel, groups, devices), out_shape=[plt...  109 us

profile of v3, /device:TPU:16, one launch (start us, length us, event | category | flops | bytes accessed | tf_op | source)
XLA Modules:
  0.0 111.6 jit_solution(8777309046098170409)
XLA Ops:
  0.6 109.0 %shard_map.77 = (bf16[2,64,4096]{2,1,0:T(8,128)(2,1)S(1)}, bf16[2,64,4096]{2,1,0:T(8,128)(2,1)S(1)}) custom-call(bf16[2,64,4096]{2,1,0:T(8,128)(2,1)} %refs_0_.1, bf16[2,64,4096]{2,1,0:T(8,128)(2,1)} %refs_1_.1, bf16[2,64,4096]{2,1,0:T(8,128)(2,1)} %refs_2_.1, bf16[2,64,4096]{2,1,0:T(8,128)(2,1)} %refs_3_.1, bf16[2,64,4096]{2,1,0:T(8,128)(2,1)} %refs_4_.1, ...), custom_call_target="tpu_custom_call" | custom-call | tf_op jit(solution)/shard_map/pallas_call | solution.py:276
  109.7 1.0 copy.10
  110.6 1.0 copy.11

commit v4 on v3

--- a/solution.py
+++ b/solution.py
@@ -102,11 +102,11 @@
         lax.fori_loop(1, devices, step, 0)
         pltpu.make_async_copy(source(me), dest, recv).start()
 
-    def send_keys(frame, part):
+    def send_keys(frame, part, size):
         for i, (source, buf) in enumerate(zip(kvs, kv_bufs)):
             send_all(
-                lambda peer: source.at[frame, pl.ds(part * half, half), head_columns(peer)],
-                buf.at[frame + 1, part, rows_of(me, half)],
+                lambda peer: source.at[frame, pl.ds(part * size, size), head_columns(peer)],
+                buf.at[frame + 1, rows_of(part * devices + me, size)],
                 kv_send.at[frame, part, i],
                 kv_recv.at[frame, part, i],
             )
@@ -115,7 +115,7 @@
         for i, (source, buf) in enumerate(zip(qs, q_bufs)):
             send_all(
                 lambda peer: source.at[frame, :, head_columns(peer)],
-                buf.at[frame, rows_of(me, tokens)],
+                buf.at[frame, rows_of(my_block * OWNERS + my_slot, tokens)],
                 q_send.at[frame, i],
                 q_recv.at[frame, i],
             )
@@ -123,9 +123,9 @@
     def await_bytes(ref, semaphore):
         pltpu.make_async_copy(ref, ref, semaphore).wait()
 
-    def await_keys(frame, part):
+    def await_keys(frame, part, size):
         for i, buf in enumerate(kv_bufs):
-            await_bytes(buf.at[frame + 1, part], kv_recv.at[frame, part, i])
+            await_bytes(buf.at[frame + 1, pl.ds(0, devices * size)], kv_recv.at[frame, part, i])
 
     def await_queries(frame):
         for i, buf in enumerate(q_bufs):
@@ -137,16 +137,20 @@
             device_id=next_place, device_id_type=MESH,
         )
 
+    my_x, my_y, my_z = me // 8, lax.rem(me // 4, 2), lax.rem(me, 4)
+    my_block = lax.rem(my_x + my_z, 4)
+    my_slot = my_x * 2 + my_y
+
     def block_of(index):
-        return lax.rem(me // OWNERS + index + 1, devices // OWNERS)
+        return lax.rem(my_block + index + 1, 4)
 
     def load_queries(frame, block):
         return [buf[frame, rows_of(block, rows)] for buf in q_bufs]
 
     def load_keys(slot, part=None):
         if part is not None:
-            return [buf[slot, part] for buf in kv_bufs]
-        return [buf[slot].reshape(width, HD) for buf in kv_bufs]
+            return [buf[slot, pl.ds(part * (width // 2), width // 2)] for buf in kv_bufs]
+        return [buf[slot] for buf in kv_bufs]
 
     def load_state(frame, block):
         place = rows_of(block, rows)
@@ -162,9 +166,11 @@
         for buf, result in zip(o_bufs, results):
             buf[frame, rows_of(block, rows)] = result
         for j in range(OWNERS):
-            owner = block * OWNERS + lax.rem(me + j, OWNERS)
+            slot = lax.rem(my_slot + j, OWNERS)
+            x, y = slot // 2, lax.rem(slot, 2)
+            owner = x * 8 + y * 4 + lax.rem(block + 4 - x, 4)
             for i, (buf, target) in enumerate(zip(o_bufs, outs)):
-                source = buf.at[frame, rows_of(owner, tokens)]
+                source = buf.at[frame, rows_of(block * OWNERS + slot, tokens)]
                 dest = target.at[frame, :, head_columns(me)]
 
                 def push():
@@ -202,23 +208,21 @@
         pl.semaphore_signal(barrier, inc=1, device_id=place, device_id_type=MESH)
     pl.semaphore_wait(barrier, devices + 1)
 
-    send_keys(1, 0)
-    send_keys(1, 1)
+    send_keys(1, 0, tokens)
     send_queries(1)
-    await_keys(1, 0)
-    await_keys(1, 1)
+    await_keys(1, 0, tokens)
     for i, buf in enumerate(kv_bufs):
         halo(i, buf).start()
-    send_keys(0, 0)
+    send_keys(0, 0, half)
     send_queries(0)
-    send_keys(0, 1)
+    send_keys(0, 1, half)
     await_queries(1)
 
     @each_block
     def _(block):
         store_state(1, block, attend(*load_queries(1, block), *load_keys(2)))
 
-    await_keys(0, 0)
+    await_keys(0, 0, half)
 
     @each_block
     def _(block):
@@ -236,7 +240,7 @@
         top, total = jnp.where(first, -1e30, top), jnp.where(first, 0.0, total)
         store_state(0, block, (top, total, *rest))
 
-    await_keys(0, 1)
+    await_keys(0, 1, half)
 
     @each_block
     def _(block):
@@ -250,10 +254,9 @@
 
     for i, buf in enumerate(kv_bufs):
         await_bytes(buf.at[2], halo_send.at[i])
-        for frame in (0, 1):
-            for part in (0, 1):
-                sent = buf.at[frame + 1, part, pl.ds(0, (devices - 1) * half)]
-                await_bytes(sent, kv_send.at[frame, part, i])
+        for frame, part, size in ((1, 0, tokens), (0, 0, half), (0, 1, half)):
+            sent = buf.at[frame + 1, pl.ds(0, (devices - 1) * size)]
+            await_bytes(sent, kv_send.at[frame, part, i])
     for i in (0, 1):
         for frame in (0, 1):
             sent = q_bufs[i].at[frame, pl.ds(0, (devices - 1) * tokens)]
@@ -267,7 +270,7 @@
     frames, tokens, model = args[0].shape
     width = tokens * devices
     bf16 = jnp.bfloat16
-    kv = pltpu.VMEM((frames + 1, 2, width // 2, HD), bf16)
+    kv = pltpu.VMEM((frames + 1, width, HD), bf16)
     q = pltpu.VMEM((frames, width, HD), bf16)
     stats = pltpu.VMEM((frames, 3, width, 1), jnp.float32)
     sums = pltpu.VMEM((frames, 3, width, HD), jnp.float32)

time: 114 us -> 110 us (0.965); the launches traced: 112 us -> 110 us
  Pallas kernels: 109 us -> 107 us
    pallas_call x1, Pallas kernels: 109 us -> 107 us  [per_device(): pl.pallas_call(functools.partial(kernel, groups, devices), out_shape=[plt...]
where the time goes in v4:
time: 110 us
  Pallas kernels  107 us (97%)
  local copies, waits for them, and re-layouts  1.94 us (2%)
    pallas_call x1, Pallas kernels, per_device(): pl.pallas_call(functools.partial(kernel, groups, devices), out_shape=[plt...  107 us

profile of v4, /device:TPU:16, one launch (start us, length us, event | category | flops | bytes accessed | tf_op | source)
XLA Modules:
  0.0 109.6 jit_solution(2001757679826714034)
XLA Ops:
  0.6 107.0 %shard_map.77 = (bf16[2,64,4096]{2,1,0:T(8,128)(2,1)S(1)}, bf16[2,64,4096]{2,1,0:T(8,128)(2,1)S(1)}) custom-call(bf16[2,64,4096]{2,1,0:T(8,128)(2,1)} %refs_0_.1, bf16[2,64,4096]{2,1,0:T(8,128)(2,1)} %refs_1_.1, bf16[2,64,4096]{2,1,0:T(8,128)(2,1)} %refs_2_.1, bf16[2,64,4096]{2,1,0:T(8,128)(2,1)} %refs_3_.1, bf16[2,64,4096]{2,1,0:T(8,128)(2,1)} %refs_4_.1, ...), custom_call_target="tpu_custom_call" | custom-call | tf_op jit(solution)/shard_map/pallas_call | solution.py:279
  107.7 1.0 copy.10
  108.6 1.0 copy.11

commit v5 on v4

--- a/solution.py
+++ b/solution.py
@@ -213,21 +213,14 @@
     await_keys(1, 0, tokens)
     for i, buf in enumerate(kv_bufs):
         halo(i, buf).start()
+    send_queries(0)
     send_keys(0, 0, half)
-    send_queries(0)
     send_keys(0, 1, half)
     await_queries(1)
 
     @each_block
     def _(block):
         store_state(1, block, attend(*load_queries(1, block), *load_keys(2)))
-
-    await_keys(0, 0, half)
-
-    @each_block
-    def _(block):
-        part = attend(*load_queries(1, block), *load_keys(1, 0))
-        store_state(1, block, join(load_state(1, block), part))
 
     await_queries(0)
     for i, buf in enumerate(kv_bufs):
@@ -239,6 +232,13 @@
         first = group == 0
         top, total = jnp.where(first, -1e30, top), jnp.where(first, 0.0, total)
         store_state(0, block, (top, total, *rest))
+
+    await_keys(0, 0, half)
+
+    @each_block
+    def _(block):
+        part = attend(*load_queries(1, block), *load_keys(1, 0))
+        store_state(1, block, join(load_state(1, block), part))
 
     await_keys(0, 1, half)
 

time: 110 us -> 110 us (level)
  no operation moved by 1% of the time
where the time goes in v5:
time: 110 us; the launch traced here: 109 us
  Pallas kernels  106 us (96%)
  local copies, waits for them, and re-layouts  1.94 us (2%)
    pallas_call x1, Pallas kernels, per_device(): pl.pallas_call(functools.partial(kernel, groups, devices), out_shape=[plt...  106 us

profile of v5, /device:TPU:16, one launch (start us, length us, event | category | flops | bytes accessed | tf_op | source)
XLA Modules:
  0.0 108.7 jit_solution(17010326343491517300)
XLA Ops:
  0.6 106.2 %shard_map.77 = (bf16[2,64,4096]{2,1,0:T(8,128)(2,1)S(1)}, bf16[2,64,4096]{2,1,0:T(8,128)(2,1)S(1)}) custom-call(bf16[2,64,4096]{2,1,0:T(8,128)(2,1)} %refs_0_.1, bf16[2,64,4096]{2,1,0:T(8,128)(2,1)} %refs_1_.1, bf16[2,64,4096]{2,1,0:T(8,128)(2,1)} %refs_2_.1, bf16[2,64,4096]{2,1,0:T(8,128)(2,1)} %refs_3_.1, bf16[2,64,4096]{2,1,0:T(8,128)(2,1)} %refs_4_.1, ...), custom_call_target="tpu_custom_call" | custom-call | tf_op jit(solution)/shard_map/pallas_call | solution.py:279
  106.8 1.0 copy.10
  107.8 1.0 copy.11
